TPU v7x, 256 devices: a whole 4x4x8 slice. The times are simulated.
256 devices in a mesh: blk: 8 (over y_lo, x), rows: 32 (over y_hi, z, core).
Axes of the slice: x: 4, y: 4 (y_hi: 2, y_lo: 2; y = y_hi * 2 + y_lo), z: 8, core: 2. Of those that a mesh axis runs over, the one named last changes fastest.
Arguments:
- embeddings: bfloat16 [524288, 768], P(('blk', 'rows')), may hold values from -6 to 6
- coverage: float32 [524288], P(('blk', 'rows')), may hold values from 0 to 4
- chosen_index: int32 [512], replicated, may hold values from 0 to 524287, as said below
- candidate_index: int32 [1024], P('blk'), may hold values from 0 to 524287, as said below
Outputs:
- new_coverage: float32 [524288], P(('blk', 'rows'))
- gains: float32 [1024], P(('blk', 'rows'))
Inputs may be any that keep to these rules, and one draw needn't show every extreme that they name: `chosen_index`: the entries are distinct; the rows r * 2048 to (r + 1) * 2048 - 1 hold at most 4 of them for every r, and exactly 4 for some r. `candidate_index`: entries b * 128 to (b + 1) * 128 - 1 lie in rows b * 65536 to (b + 1) * 65536 - 1.
All inputs are finite; a program needn't handle non-finite values.
Results may differ from a plain program's by a relative error of at most 0.00035.
Values may be sent and summed in bfloat16 or wider, within the bound.
No kernel may reach another device: no remote copies, remote signals or barrier semaphores. Data moves between devices by JAX's collectives and lax.ppermute only.
A program may use at most 64 MiB of HBM per device.

v0:
```python
import jax
import jax.numpy as jnp
from jax import lax
from jax.sharding import Mesh
from jax.sharding import PartitionSpec as P

BLK = ("blk_0", "blk_1")
BLK_ROWS = ("blk_0", "blk_1", "rows")


def in_order(pieces, dim):
    pieces = jnp.moveaxis(pieces, 0, dim)
    dims = pieces.shape
    return pieces.reshape(*dims[:dim], dims[dim] * dims[dim + 1], *dims[dim + 2 :])


def all_blocks(x, axes, sequence):
    pieces = x[None]
    for k in sequence:
        pieces = lax.all_gather(pieces, axes[k], axis=0, tiled=True)
    held = [lax.axis_size(axes[k]) for k in reversed(sequence)]
    pieces = pieces.reshape(*held, *x.shape)
    turned = sorted(range(len(sequence)), key=lambda place: sequence[len(sequence) - 1 - place])
    return pieces.transpose(*turned, *range(len(sequence), pieces.ndim)).reshape(-1, *x.shape)


def whole_of(x, axes, sequence, dim):
    return in_order(all_blocks(x, axes, sequence), dim)


def owned_rows(embeddings, indices, base_row):
    local_rows = embeddings.shape[0]
    offset = indices - base_row
    inside = (offset >= 0) & (offset < local_rows)
    safe = jnp.clip(offset, 0, local_rows - 1)
    picked = jnp.take(embeddings, safe, axis=0).astype(jnp.float32)
    return jnp.where(inside[:, None], picked, 0.0)


def local(embeddings, coverage, chosen_index, candidate_index):
    local_rows = embeddings.shape[0]
    width = embeddings.shape[1]
    scale = 1.0 / width**0.5
    device_pos = lax.axis_index(BLK) * lax.axis_size("rows") + lax.axis_index("rows")
    base_row = device_pos * local_rows
    chosen_f = lax.psum(owned_rows(embeddings, chosen_index, base_row), BLK_ROWS)
    chosen_rows = chosen_f.astype(jnp.bfloat16)
    sims = jnp.dot(embeddings, chosen_rows.T, preferred_element_type=jnp.float32) * scale
    best = jnp.max(sims, axis=1)
    new_coverage = jnp.maximum(coverage, best)
    every_index = whole_of(candidate_index, BLK, (0, 1), 0)
    every_f = lax.psum(owned_rows(embeddings, every_index, base_row), BLK_ROWS)
    every_rows = every_f.astype(jnp.bfloat16)
    cand_sims = jnp.dot(embeddings, every_rows.T, preferred_element_type=jnp.float32) * scale
    gain_part = jnp.sum(jnp.maximum(cand_sims - new_coverage[:, None], 0.0), axis=0)
    gains = lax.psum_scatter(gain_part, BLK_ROWS, scatter_dimension=0, tiled=True)
    return (new_coverage, gains)


def solution(mesh):
    torus = Mesh(mesh.devices.reshape(2, 4, mesh.shape["rows"]), ("blk_0", "blk_1", "rows"))
    return jax.shard_map(
        local,
        mesh=torus,
        in_specs=(P(BLK_ROWS, None), P(BLK_ROWS), P(), P(BLK)),
        out_specs=(P(BLK_ROWS), P(BLK_ROWS)),
        check_vma=False,
    )
```

profile of v0, /device:TPU:1, one launch (start us, length us, event | category | flops | bytes accessed | tf_op | source)
XLA Modules:
  0.0 248.3 jit_solution(17189368050249611175)
XLA Ops:
  0.6 0.0 copy-start
  0.7 0.8 compare_and_fusion.1
  1.5 1.0 copy-done
  2.5 0.0 copy-start.4
  2.5 2.7 %gather_fusion = bf16[512,768]{1,0:T(8,128)(2,1)} fusion(bf16[2048,768]{1,0:T(8,128)(2,1)S(1)} %copy-done, s32[1024]{0:T(1024)S(1)} %pad_clamp_fusion), kind=kCustom, calls=%fused_computation | custom fusion | bytes 1574912 | tf_op jit(solution)/shard_map/jit(_take)/gather | solution.py:36
  5.2 2.5 %convert_select_fusion.1 = f32[512,768]{1,0:T(8,128)} fusion(bf16[512,768]{1,0:T(8,128)(2,1)} %gather_fusion, pred[512]{0:T(512)(128)(4,1)S(1)} %get-tuple-element.4, pred[512]{0:T(512)(128)(4,1)S(1)} %get-tuple-element.6), kind=kLoop, calls=%fused_computation.6 | loop fusion | flops 1179648 | bytes 2360320 | tf_op jit(solution)/shard_map/jit(_where)/select_n | solution.py:37
  7.8 0.0 copy-done.4
  7.8 3.7 %all-gather.1 = s32[2,1,128]{2,1,0:T(1,128)S(1)} all-gather(s32[1,1,128]{2,1,0:T(1,128)S(1)} %bitcast.19), channel_id=2, replica_groups=mesh['blk_0'=2,'blk_1'=4,'rows'=32] {'blk_0'}, dimensions={0}, use_global_device_ids=true | all-gather | bytes 1536 | tf_op jit(solution)/shard_map/all_gather | solution.py:20
  11.5 7.9 %all-gather.2 = s32[4,2,128]{2,1,0:T(2,128)S(1)} all-gather(s32[1,2,128]{2,1,0:T(2,128)S(1)} %bitcast.18), channel_id=1, replica_groups=mesh['blk_0'=2,'blk_1'=4,'rows'=32] {'blk_1'}, dimensions={0}, use_global_device_ids=true | all-gather | bytes 5120 | tf_op jit(solution)/shard_map/all_gather | solution.py:20
  19.4 5.2 %gather_fusion.1 = bf16[1024,768]{1,0:T(8,128)(2,1)} fusion(bf16[2048,768]{1,0:T(8,128)(2,1)S(1)} %copy-done, s32[1024]{0:T(1024)S(1)} %broadcast_clamp_fusion), kind=kCustom, calls=%fused_computation.1 | custom fusion | bytes 3149824 | tf_op jit(solution)/shard_map/jit(_take)/gather | solution.py:36
  24.7 3.2 %convert_select_fusion = f32[1024,768]{1,0:T(8,128)} fusion(bf16[1024,768]{1,0:T(8,128)(2,1)} %gather_fusion.1, pred[1024]{0:T(1024)(128)(4,1)S(1)} %compare_and_fusion, pred[1024]{0:T(1024)(128)(4,1)S(1)} %bitcast.17), kind=kLoop, calls=%fused_computation.4 | loop fusion | flops 2359296 | bytes 4720640 | tf_op jit(solution)/shard_map/jit(_where)/select_n | solution.py:37
  27.9 138.1 %all-reduce.3 = (bf16[512,768]{1,0:T(8,128)(2,1)}, bf16[1024,768]{1,0:T(8,128)(2,1)}) all-reduce(f32[512,768]{1,0:T(8,128)} %convert_select_fusion.1, f32[1024,768]{1,0:T(8,128)} %convert_select_fusion), channel_id=1, replica_groups=mesh['blk_0'=2,'blk_1'=4,'rows'=32] {'blk_0','blk_1','rows'}, use_global_device_ids=true, to_apply=%region_0.1 | all-reduce | flops 1179648 | bytes 7077888 | tf_op jit(solution)/shard_map/psum | solution.py:46
  166.0 0.0 copy-start.1
  166.0 0.0 copy-start.3
  166.0 3.1 %multiply_reduce_fusion = f32[2048]{0:T(1024)S(1)} fusion(bf16[2048,768]{1,0:T(8,128)(2,1)S(1)} %copy-done, bf16[512,768]{1,0:T(8,128)(2,1)} %get-tuple-element.2), kind=kOutput, calls=%fused_computation.3 | convolution fusion | flops 1612707840 | bytes 3940352 | tf_op jit(solution)/shard_map/dot_general | solution.py:48
  169.1 0.0 copy-done.1
  169.1 0.0 copy-start.2
  169.2 0.0 copy-done.3
  169.2 3.9 %maximum_reduce_fusion = f32[1024]{0:T(1024)S(1)} fusion(bf16[2048,768]{1,0:T(8,128)(2,1)S(1)} %copy-done, f32[2048]{0:T(1024)S(1)} %max.18, bf16[1024,768]{1,0:T(8,128)(2,1)S(1)} %copy-done.3), kind=kOutput, calls=%fused_computation.2 | convolution fusion | flops 3229613056 | bytes 4730880 | tf_op jit(solution)/shard_map/dot_general | solution.py:54
  173.0 0.0 copy-done.2
  173.0 74.7 %all-reduce = f32[1024]{0:T(1024)S(1)} all-reduce(f32[1024]{0:T(1024)S(1)} %maximum_reduce_fusion), channel_id=3, replica_groups=mesh['blk_0'=2,'blk_1'=4,'rows'=32] {'blk_0','blk_1','rows'}, use_global_device_ids=true, to_apply=%region_4.5.clone | all-reduce | flops 1024 | bytes 8192
  247.8 0.6 dynamic-slice
  (9 shorter events, 0.1 us)
Async XLA Ops:
  0.6 1.9 copy-start
  2.5 5.3 %copy-start.4 = (s32[128]{0:T(128)S(1)}, s32[128]{0:T(128)}, u32[]{:S(2)}) copy-start(s32[128]{0:T(128)} %param.7) | copy-start | bytes 1540
  166.0 3.1 %copy-start.1 = (f32[2048]{0:T(1024)S(1)}, f32[2048]{0:T(1024)}, u32[]{:S(2)}) copy-start(f32[2048]{0:T(1024)} %param.5) | copy-start | bytes 24580
  166.0 3.1 %copy-start.3 = (bf16[1024,768]{1,0:T(8,128)(2,1)S(1)}, bf16[1024,768]{1,0:T(8,128)(2,1)}, u32[]{:S(2)}) copy-start(bf16[1024,768]{1,0:T(8,128)(2,1)} %get-tuple-element.3) | copy-start | bytes 4718596
  169.1 3.9 %copy-start.2 = (f32[2048]{0:T(1024)}, f32[2048]{0:T(1024)S(1)}, u32[]{:S(2)}) copy-start(f32[2048]{0:T(1024)S(1)} %max.18) | copy-start | bytes 24580
where the time goes:
time: 249 us; the launch traced here: 248 us
  blocking collectives  224 us (90%)
  local copies, waits for them, and re-layouts  9.6 us (4%)
  matrix products  6.95 us (3%)
  other arithmetic  6.67 us (3%)
    psum x1, blocking collectives, local(): lax.psum(owned_rows(embeddings, chosen_index, base_row), BLK_ROWS)  138 us
    unnamed x1, blocking collectives  74.7 us
    all_gather x2, blocking collectives, all_blocks(): pieces = lax.all_gather(pieces, axes[k], axis=0, tiled=True)  11.6 us
    gather x2, local copies, waits for them, and re-layouts, owned_rows(): picked = jnp.take(embeddings, safe, axis=0).astype(jnp.float32)  7.95 us
    select_n x2, other arithmetic, owned_rows(): return jnp.where(inside[:, None], picked, 0.0)  5.78 us

commit v1 on v0

--- a/solution.py
+++ b/solution.py
@@ -43,7 +43,9 @@
     scale = 1.0 / width**0.5
     device_pos = lax.axis_index(BLK) * lax.axis_size("rows") + lax.axis_index("rows")
     base_row = device_pos * local_rows
-    chosen_f = lax.psum(owned_rows(embeddings, chosen_index, base_row), BLK_ROWS)
+    chosen_f = lax.psum(
+        lax.psum(owned_rows(embeddings, chosen_index, base_row), ("blk_1", "rows")), "blk_0"
+    )
     chosen_rows = chosen_f.astype(jnp.bfloat16)
     sims = jnp.dot(embeddings, chosen_rows.T, preferred_element_type=jnp.float32) * scale
     best = jnp.max(sims, axis=1)

time: 249 us -> 1370 us (5.50)
  waiting for transfers between devices: 0 us -> 1070 us
  blocking collectives: 224 us -> 259 us
    psum x0 -> x1, waiting for transfers between devices: none -> 1070 us  [local(): lax.psum(owned_rows(embeddings, chosen_index, base_row), ('blk_1', 'rows'))]
    psum x1 -> x2, blocking collectives: 138 us -> 171 us  [the longest x1 134 us: local(): every_f = lax.psum(owned_rows(embeddings, every_index, base_row), BLK_ROWS)]
  transfers between devices with their start and end apart: 0 -> 1, of which waited for: 0 -> 1; matrix products, arithmetic and copies ran while one was open for 0% -> 1% of each run, Pallas kernels for 0% -> 0%
where the time goes in v1:
time: 1370 us
  waiting for transfers between devices  1070 us (78%)
  blocking collectives  259 us (19%)
  between operations  14.1 us (1%)
    psum x1, waiting for transfers between devices, local(): lax.psum(owned_rows(embeddings, chosen_index, base_row), ('blk_1', 'rows'))  1070 us
    psum x1, blocking collectives, local(): every_f = lax.psum(owned_rows(embeddings, every_index, base_row), BLK_ROWS)  134 us
    unnamed x1, blocking collectives  77 us
    psum x1, blocking collectives, local(): lax.psum(lax.psum(owned_rows(embeddings, chosen_index, base_row), ('blk_1...  36.2 us
  transfers between devices with their start and end apart: 1, of which 1 were waited for; matrix products, arithmetic and copies ran while one was open for 1% of the time, Pallas kernels for 0%

profile of v1, /device:TPU:1, one launch (start us, length us, event | category | flops | bytes accessed | tf_op | source)
XLA Modules:
  0.0 1369.7 jit_solution(5874132732941255776)
XLA Ops:
  7.2 0.0 copy-start
  7.2 0.0 all-reduce.5.cloned.1.call-start
  7.2 0.8 compare_and_fusion.1
  8.1 1.0 copy-done
  9.1 2.7 gather_fusion
  11.8 0.0 copy-start.4
  11.8 2.6 convert_select_fusion.1
  14.4 0.0 all-reduce.5.cloned.1.call-update
  14.4 0.0 copy-done.4
  14.4 3.7 all-gather.1
  18.1 7.9 all-gather.2
  26.1 5.2 gather_fusion.1
  31.3 3.2 convert_select_fusion
  34.5 134.4 %all-reduce.7 = bf16[1024,768]{1,0:T(8,128)(2,1)} all-reduce(f32[1024,768]{1,0:T(8,128)} %convert_select_fusion), channel_id=1, replica_groups=mesh['blk_0'=2,'blk_1'=4,'rows'=32] {'blk_0','blk_1','rows'}, use_global_device_ids=true, to_apply=%region_3.4 | all-reduce | flops 786432 | bytes 4718592 | tf_op jit(solution)/shard_map/psum | solution.py:54
  169.0 1073.1 %all-reduce.5.cloned.1.call-done = f32[512,768]{1,0:T(8,128)} async-done(((f32[512,768]{1,0:T(8,128)}), f32[512,768]{1,0:T(8,128)}) %all-reduce.5.cloned.1.call-update) | async-done | bytes 1572880 | tf_op jit(solution)/shard_map/psum | solution.py:47
  1242.1 36.2 %all-reduce.6 = bf16[512,768]{1,0:T(8,128)(2,1)} all-reduce(f32[512,768]{1,0:T(8,128)} %all-reduce.5.cloned.1.call-done), channel_id=1, replica_groups=mesh['blk_0'=2,'blk_1'=4,'rows'=32] {'blk_0'}, use_global_device_ids=true, to_apply=%region_1.2 | all-reduce | flops 393216 | bytes 2359296 | tf_op jit(solution)/shard_map/psum | solution.py:46
  1278.3 0.0 copy-start.2
  1278.3 0.0 copy-start.1
  1278.3 3.1 multiply_reduce_fusion
  1281.4 0.0 copy-done.2
  1281.4 0.0 copy-done.1
  1281.4 0.0 copy-start.3
  1281.5 3.9 maximum_reduce_fusion
  1285.3 0.0 copy-done.3
  1285.3 77.0 %all-reduce = f32[1024]{0:T(1024)S(1)} all-reduce(f32[1024]{0:T(1024)S(1)} %maximum_reduce_fusion), channel_id=3, replica_groups=mesh['blk_0'=2,'blk_1'=4,'rows'=32] {'blk_0','blk_1','rows'}, use_global_device_ids=true, to_apply=%region_5.6.clone | all-reduce | flops 1024 | bytes 8192
  1362.3 0.6 dynamic-slice
  (9 shorter events, 0.1 us)
Async XLA Ops:
  7.2 1.9 copy-start
  7.2 1234.9 %all-reduce.5.cloned.1.call-start = ((), (), s32[]{:S(2)}) async-start(), calls=%async_computation | async-start | bytes 3145728 | tf_op jit(solution)/shard_map/psum | solution.py:47
  11.8 2.6 copy-start.4
  1278.3 3.1 copy-start.2
  1278.3 3.1 copy-start.1
  1281.4 3.9 copy-start.3
Sparse Core Ops, SparseCore 0:
  14.5 1227.4 all-reduce.4
